TPU v7x, 32 devices: a whole 2x2x4 slice. The times are simulated.
32 devices in a mesh: tm: 4 (over y, x), space: 8 (over z, core).
Axes of the slice: x: 2, y: 2, z: 4, core: 2. Of those that a mesh axis runs over, the one named last changes fastest.
Arguments:
- anomalies: bfloat16 [16, 128, 32768], P('tm', None, 'space'), may hold values from -51 to 51
- obs_index: int32 [16, 8192], P('tm', 'space'), may hold values from 0 to 4095
- obs_weight: float32 [16, 8192], P('tm', 'space'), may hold values from 0.01 to 0.12
Outputs:
- smoothed: bfloat16 [16, 128, 32768], P('tm', None, 'space')
All inputs are finite; a program needn't handle non-finite values.
Results may differ from a plain program's by a relative error of at most 0.0034.
Values sent between devices are 32-bit elements; how exact they have to be, the bound alone decides.
A program may use at most 64 MiB of HBM per device.

v0:
```python
import jax
import jax.numpy as jnp
from jax import lax
from jax.sharding import PartitionSpec as P


def carried_in(part, axis, combine, identity):
    count = lax.axis_size(axis)
    place = lax.axis_index(axis)
    ahead = count - 1 - place
    gathered = lax.all_gather(part, axis)
    state = jnp.zeros_like(part) + jnp.asarray(identity, part.dtype)

    def one(step, state):
        source = count - 1 - step
        return combine(state, lax.dynamic_index_in_dim(gathered, source, 0, False))

    return lax.fori_loop(0, ahead, one, state)


def transform(gram_total, spread_dof, identity):
    factor = jnp.linalg.cholesky(spread_dof * identity + gram_total)
    inverse_low = lax.linalg.triangular_solve(
        factor, jnp.broadcast_to(identity, gram_total.shape), left_side=True, lower=True
    )
    return spread_dof * jnp.einsum(
        "tkm,tkn->tmn", inverse_low, inverse_low, precision=lax.Precision.HIGHEST
    )


def advance(running, weight_now):
    return (jnp.dot(weight_now, running, precision=lax.Precision.HIGHEST), running)


def pick_cells(anomalies, obs_index):
    grid_cells = anomalies.shape[2]
    cell_ids = lax.broadcasted_iota(jnp.int32, (1, 1, grid_cells), 2)
    selector = (obs_index[:, :, None] == cell_ids).astype(jnp.bfloat16)
    return jnp.einsum("tmc,toc->tmo", anomalies, selector, preferred_element_type=jnp.float32)


def per_device(anomalies, obs_index, obs_weight):
    local_times, member_count, grid_cells = anomalies.shape
    spread_dof = float(member_count - 1)
    identity = jnp.eye(member_count, dtype=jnp.float32)
    picked = pick_cells(anomalies, obs_index)
    scaled = (picked * obs_weight[:, None, :]).astype(jnp.bfloat16)
    gram_part = jnp.einsum("tmo,tno->tmn", scaled, scaled, preferred_element_type=jnp.float32)
    summed = lax.psum(gram_part, "space")
    weights = transform(summed, spread_dof, identity)
    own_product = identity
    for position in range(local_times):
        own_product = jnp.dot(own_product, weights[position], precision=lax.Precision.HIGHEST)

    def compose(earlier, later_one):
        return jnp.dot(later_one, earlier, precision=lax.Precision.HIGHEST)

    suffix = carried_in(own_product, "tm", compose, identity)
    _, chains = lax.scan(advance, suffix, weights, reverse=True)
    chains_low = chains.astype(jnp.bfloat16)
    smoothed = jnp.einsum("tmn,tmc->tnc", chains_low, anomalies, preferred_element_type=jnp.float32)
    return smoothed.astype(jnp.bfloat16)


def solution(mesh):
    return jax.shard_map(
        per_device,
        mesh=mesh,
        in_specs=(P("tm", None, "space"), P("tm", "space"), P("tm", "space")),
        out_specs=P("tm", None, "space"),
        check_vma=False,
    )
```

profile of v0, /device:TPU:0, one launch (start us, length us, event | category | flops | bytes accessed | tf_op | source)
XLA Modules:
  0.0 209.9 jit_solution(3842327023063733566)
XLA Ops:
  6.5 0.0 all-reduce.2.cloned.1.call-start
  6.5 31.2 %fusion.10 = f32[4,128,128]{1,2,0:T(8,128)} fusion(bf16[4,128,4096]{2,1,0:T(8,128)(2,1)} %param.7, s32[4,1024]{1,0:T(4,128)} %param.8, f32[4,1024]{1,0:T(4,128)} %param.9), kind=kOutput, calls=%fused_computation.15 | convolution fusion | flops 4447010816 | bytes 4489216 | tf_op jit(solution)/shard_map/tmo,tno->tmn/dot_general | solution.py:48
  37.7 0.0 all-reduce.2.cloned.1.call-update
  37.8 0.1 copy.10
  37.9 57.6 %all-reduce.2.cloned.1.call-done = f32[4,128,128]{1,2,0:T(8,128)} async-done(((f32[4,128,128]{1,2,0:T(8,128)}), f32[4,128,128]{1,2,0:T(8,128)}) %all-reduce.2.cloned.1.call-update) | async-done | bytes 262160 | tf_op jit(solution)/shard_map/psum | solution.py:49
  95.5 1.0 broadcast_add_fusion
  96.5 0.1 copy.13
  96.6 1.0 fusion.13
  97.6 46.9 %custom-call.7 = f32[4,128,128]{2,1,0:T(8,128)S(1)} custom-call(f32[4,128,128]{2,1,0:T(8,128)S(1)} %fusion.13), custom_call_target="Cholesky" | custom-call | tf_op jit(solution)/shard_map/jit(cholesky)/cholesky | solution.py:22
  144.6 0.1 compare_reduce_fusion
  144.7 0.1 select_bitcast_fusion
  144.8 39.5 %custom-call.8 = f32[4,1,128,128]{2,3,1,0:T(8,128)S(1)} custom-call(f32[4,1,128,128]{3,2,1,0:T(8,128)S(1)} %select_bitcast_fusion), custom_call_target="InvertDiagBlocksLowerTriangular" | custom-call | tf_op jit(solution)/shard_map/triangular_solve | solution.py:23
  184.3 0.6 fusion.11
  184.9 0.7 convolution_multiply_fusion
  185.6 0.2 fusion.19
  185.7 0.2 fusion.18
  186.0 0.2 fusion.17
  186.2 0.2 fusion.16
  186.4 9.3 %all-gather = f32[512,128]{1,0:T(8,128)S(1)} all-gather(f32[128,128]{1,0:T(8,128)S(1)} %fusion.16), channel_id=2, replica_groups=mesh['tm'=4,'space'=8] {'tm'}, dimensions={0}, use_global_device_ids=true | all-gather | bytes 327680 | tf_op jit(solution)/shard_map/all_gather | solution.py:11
  195.7 0.7 while.28
  195.7 0.2 fusion.40
  195.9 0.2 fusion.40
  196.2 0.2 fusion.40
  196.4 1.1 while.29
  196.5 0.2 fusion.43
  196.8 0.2 fusion.43
  197.0 0.2 fusion.43
  197.3 0.2 fusion.43
  197.5 5.5 %convolution_convert_fusion = bf16[4,128,4096]{2,1,0:T(8,128)(2,1)} fusion(bf16[4,128,4096]{2,1,0:T(8,128)(2,1)} %param.7, bf16[4,128,128]{2,1,0:T(8,128)(2,1)S(1)} %get-tuple-element.146), kind=kOutput, calls=%fused_computation.12 | convolution fusion | flops 538968064 | bytes 8519680 | tf_op jit(solution)/shard_map/tmn,tmc->tnc/dot_general | solution.py:61
  (17 shorter events, 0.2 us)
Async XLA Ops:
  6.5 89.0 %all-reduce.2.cloned.1.call-start = ((), (), s32[]{:S(2)}) async-start(), calls=%async_computation | async-start | bytes 524288 | tf_op jit(solution)/shard_map/psum | solution.py:49
Sparse Core Ops, SparseCore 0:
  37.8 57.6 all-reduce.1
where the time goes:
time: 210 us
  other arithmetic  88.7 us (42%)
  waiting for transfers between devices  57.6 us (27%)
  matrix products  40.1 us (19%)
  between operations  13.5 us (6%)
  blocking collectives  9.3 us (4%)
    psum x1, waiting for transfers between devices, per_device(): summed = lax.psum(gram_part, 'space')  57.6 us
    another operation x3, other arithmetic, transform(): factor = jnp.linalg.cholesky(spread_dof * identity + gram_total)  47.1 us
    another operation x3, other arithmetic, transform(): lax.linalg.triangular_solve(factor, jnp.broadcast_to(identity, gram_total...  39.6 us
    dot_general x1, matrix products, per_device(): jnp.einsum('tmo,tno->tmn', scaled, scaled, preferred_element_type=jnp.flo...  31.2 us
    all_gather x1, blocking collectives, carried_in(): gathered = lax.all_gather(part, axis)  9.3 us
    dot_general x1, matrix products, per_device(): jnp.einsum('tmn,tmc->tnc', chains_low, anomalies, preferred_element_type=...  5.49 us
  transfers between devices with their start and end apart: 1, of which 1 were waited for; matrix products, arithmetic and copies ran while one was open for 0% of the time, Pallas kernels for 0%

commit v1 on v0

v1 whole, which is shorter than its diff:
```python
import functools
import math

import jax
import jax.numpy as jnp
from jax import lax
from jax.experimental import pallas as pl
from jax.experimental.pallas import tpu as pltpu
from jax.sharding import PartitionSpec as P

MESH = pl.DeviceIdType.MESH
HIGHEST = lax.Precision.HIGHEST
GROUPS = 4
LARGEST_SCALED = 51.0 * 0.12


def exact_dot(left, right):
    return jnp.dot(left, right, precision=HIGHEST, preferred_element_type=jnp.float32)


def gram_kernel(anomalies_ref, index_ref, weight_ref, gram_ref):
    time = pl.program_id(0)
    members, cells = anomalies_ref.shape[1:]
    obs = index_ref.shape[1]
    span = cells // GROUPS
    shift = span.bit_length() - 1
    chunk = 256 if obs % 256 == 0 else obs
    index = index_ref[pl.ds(time, 1), :]
    weight = weight_ref[pl.ds(time, 1), :]
    low = jnp.bitwise_and(index, span - 1)
    high = lax.shift_right_logical(index, shift)
    stacked = jnp.concatenate(
        [anomalies_ref[0, :, g * span:(g + 1) * span] for g in range(GROUPS)], axis=0
    )
    cell_ids = lax.broadcasted_iota(jnp.int32, (span, chunk), 0)
    total = jnp.zeros((members, members), jnp.float32)
    for start in range(0, obs, chunk):
        part = slice(start, start + chunk)
        selector = (cell_ids == low[:, part]).astype(jnp.float32).astype(jnp.bfloat16)
        picked = jnp.dot(stacked, selector, preferred_element_type=jnp.float32)
        scaled = jnp.zeros((members, chunk), jnp.float32)
        for g in range(GROUPS):
            group_weight = jnp.where(high[:, part] == g, weight[:, part], 0.0)
            scaled = scaled + picked[g * members:(g + 1) * members] * group_weight
        scaled = scaled.astype(jnp.bfloat16)
        total = total + lax.dot_general(
            scaled, scaled, (((1,), (1,)), ((), ())), preferred_element_type=jnp.float32
        )
    gram_ref[0] = total


def inverse_of(matrix, identity, steps, both_ref):
    norm = jnp.max(jnp.sum(jnp.abs(matrix), axis=1, keepdims=True), axis=0, keepdims=True)
    least = 1.0 / norm
    size = matrix.shape[0]
    both_ref[:size] = matrix * least
    both_ref[size:] = identity * least

    def step(_, least):
        alpha = 2.0 / (1.0 + least)
        factor = (2.0 * alpha) * identity - (alpha * alpha) * both_ref[:size]
        both_ref[...] = exact_dot(both_ref[...], factor)
        return 4.0 * least / ((1.0 + least) * (1.0 + least))

    lax.fori_loop(0, steps, step, least)
    return both_ref[size:]


def tree(items):
    while len(items) > 1:
        paired = [exact_dot(a, b) for a, b in zip(items[::2], items[1::2])]
        items = paired + items[len(items) - len(items) % 2:]
    return items[0]


def chain_kernel(space, tm, times, steps, gram_ref, out_ref, landed, matrix, weights, products, both_ref,
                 scatter_send, scatter_recv, share_send, share_recv, spread_send, spread_recv,
                 pass_send, pass_recv, time_send, time_recv, relay_send, relay_recv):
    members = matrix.shape[0]
    me = lax.axis_index("space")
    mine = lax.axis_index("tm")
    rows = times * members // space
    team = space // times
    owned = me // team
    place = me % team
    base = owned * team

    def row_slice(number):
        return pl.ds(pl.multiple_of(number * rows, rows), rows)

    def to(source, target, send, recv, **device):
        return pltpu.make_async_remote_copy(
            src_ref=source, dst_ref=target, send_sem=send, recv_sem=recv,
            device_id=device, device_id_type=MESH,
        )

    barrier = pltpu.get_barrier_semaphore()
    for d in range(1, space):
        pl.semaphore_signal(barrier, inc=1, device_id={"space": (me + d) % space}, device_id_type=MESH)
    for d in range(1, tm):
        pl.semaphore_signal(barrier, inc=1, device_id={"tm": (mine + d) % tm}, device_id_type=MESH)
    pl.semaphore_wait(barrier, space + tm - 2)

    sends = []
    for d in range(1, space):
        peer = (me + d) % space
        copy = to(gram_ref.at[row_slice(peer)], landed.at[d], scatter_send.at[d],
                  scatter_recv.at[d], space=peer)
        copy.start()
        sends.append(copy)
    for copy in sends:
        copy.wait_recv()
    total = gram_ref[row_slice(me), :]
    for d in range(1, space):
        total = total + landed[d]
    matrix[row_slice(place), :] = total
    shares = []
    for d in range(1, team):
        peer = (place + d) % team
        copy = to(matrix.at[row_slice(place)], matrix.at[row_slice(place)], share_send.at[d],
                  share_recv.at[d], space=base + peer)
        copy.start()
        shares.append(copy)
    for d in range(1, team):
        origin = (place + team - d) % team
        to(matrix.at[row_slice(origin)], matrix.at[row_slice(origin)], share_send.at[d],
           share_recv.at[d], space=base + origin).wait_recv()

    identity = (
        lax.broadcasted_iota(jnp.int32, (members, members), 0)
        == lax.broadcasted_iota(jnp.int32, (members, members), 1)
    ).astype(jnp.float32)
    spread = float(members - 1)
    weights[owned] = inverse_of(identity + matrix[...] / spread, identity, steps, both_ref)

    def own_rows(slot):
        return weights.at[slot, row_slice(place)]

    for d in range(1, times):
        copy = to(own_rows(owned), own_rows(owned), spread_send.at[d], spread_recv.at[d],
                  space=((owned + d) % times) * team + place)
        copy.start()
        sends.append(copy)
    for d in range(1, times):
        slot = (owned + times - d) % times
        to(own_rows(slot), own_rows(slot), spread_send.at[d], spread_recv.at[d],
           space=slot * team + place).wait_recv()
        for e in range(1, team):
            copy = to(own_rows(slot), own_rows(slot), pass_send.at[d, e], pass_recv.at[d, e],
                      space=base + (place + e) % team)
            copy.start()
            sends.append(copy)
    for d in range(1, times):
        slot = (owned + times - d) % times
        for e in range(1, team):
            origin = (place + team - e) % team
            there = weights.at[slot, row_slice(origin)]
            to(there, there, pass_send.at[d, e], pass_recv.at[d, e], space=base + origin).wait_recv()

    each = [weights[t] for t in range(times)]
    products[mine] = tree(each)

    def product_rows(slot, number):
        return products.at[slot, row_slice(number)]

    for d in range(1, tm):
        @pl.when(mine >= d)
        def _(d=d):
            to(product_rows(mine, place), product_rows(mine, place), time_send.at[d],
               time_recv.at[d], tm=jnp.maximum(mine - d, 0)).start()

    tails = [identity]
    for t in range(times - 1, 0, -1):
        tails.append(exact_dot(each[t], tails[-1]) if t < times - 1 else each[t])
    tails = tails[::-1]

    for d in range(1, tm):
        @pl.when(mine + d < tm)
        def _(d=d):
            slot = jnp.minimum(mine + d, tm - 1)
            to(product_rows(slot, place), product_rows(slot, place), time_send.at[d],
               time_recv.at[d], tm=slot).wait_recv()
            for e in range(1, team):
                to(product_rows(slot, place), product_rows(slot, place), relay_send.at[d, e],
                   relay_recv.at[d, e], space=base + (place + e) % team).start()
    for d in range(1, tm):
        @pl.when(mine + d < tm)
        def _(d=d):
            slot = jnp.minimum(mine + d, tm - 1)
            for e in range(1, team):
                origin = (place + team - e) % team
                to(product_rows(slot, origin), product_rows(slot, origin), relay_send.at[d, e],
                   relay_recv.at[d, e], space=base + origin).wait_recv()

    later = [jnp.where(slot > mine, products[slot], identity) for slot in range(1, tm)]
    suffix = tree(later) if later else identity
    chains = exact_dot(jnp.concatenate(tails, axis=0), suffix)
    for t in range(times):
        out_ref[t] = chains[t * members:(t + 1) * members].T.astype(out_ref.dtype)

    for copy in sends + shares:
        copy.wait_send()
    for d in range(1, tm):
        @pl.when(mine >= d)
        def _(d=d):
            to(product_rows(mine, place), product_rows(mine, place), time_send.at[d],
               time_recv.at[d], tm=jnp.maximum(mine - d, 0)).wait_send()

        @pl.when(mine + d < tm)
        def _(d=d):
            slot = jnp.minimum(mine + d, tm - 1)
            for e in range(1, team):
                to(product_rows(slot, place), product_rows(slot, place), relay_send.at[d, e],
                   relay_recv.at[d, e], space=base + (place + e) % team).wait_send()


def smooth_kernel(chain_ref, anomalies_ref, out_ref):
    out_ref[0] = jnp.dot(
        chain_ref[0], anomalies_ref[0], preferred_element_type=jnp.float32
    ).astype(out_ref.dtype)


def per_device(space, tm, anomalies, obs_index, obs_weight):
    times, members, cells = anomalies.shape
    obs = obs_index.shape[1]
    whole_vmem = pl.BlockSpec(memory_space=pltpu.VMEM)
    one_time = pl.BlockSpec((1, members, cells), lambda t: (t, 0, 0))
    square = pl.BlockSpec((1, members, members), lambda t: (t, 0, 0))
    gram = pl.pallas_call(
        gram_kernel,
        grid=(times,),
        in_specs=[one_time, whole_vmem, whole_vmem],
        out_specs=square,
        out_shape=jax.ShapeDtypeStruct((times, members, members), jnp.float32),
        compiler_params=pltpu.CompilerParams(vmem_limit_bytes=40 * 2**20),
    )(anomalies, obs_index, obs_weight)

    bound = 1.0 + members * obs * space * LARGEST_SCALED**2 / (members - 1)
    steps = math.ceil(math.log(bound / 4.0, 4)) + 4
    rows = times * members // space
    team = space // times
    dma = pltpu.SemaphoreType.DMA
    chains = pl.pallas_call(
        functools.partial(chain_kernel, space, tm, times, steps),
        in_specs=[whole_vmem],
        out_specs=whole_vmem,
        out_shape=jax.ShapeDtypeStruct((times, members, members), jnp.bfloat16),
        scratch_shapes=[
            pltpu.VMEM((space, rows, members), jnp.float32),
            pltpu.VMEM((members, members), jnp.float32),
            pltpu.VMEM((times, members, members), jnp.float32),
            pltpu.VMEM((tm, members, members), jnp.float32),
            pltpu.VMEM((2 * members, members), jnp.float32),
            dma((space,)), dma((space,)), dma((team,)), dma((team,)), dma((times,)), dma((times,)),
            dma((times, team)), dma((times, team)), dma((tm,)), dma((tm,)),
            dma((tm, team)), dma((tm, team)),
        ],
        compiler_params=pltpu.CompilerParams(
            collective_id=0, has_side_effects=True, vmem_limit_bytes=40 * 2**20
        ),
    )(gram.reshape(times * members, members))

    return pl.pallas_call(
        smooth_kernel,
        grid=(times,),
        in_specs=[square, one_time],
        out_specs=one_time,
        out_shape=jax.ShapeDtypeStruct(anomalies.shape, anomalies.dtype),
        compiler_params=pltpu.CompilerParams(vmem_limit_bytes=40 * 2**20),
    )(chains, anomalies)


def solution(mesh):
    return jax.shard_map(
        functools.partial(per_device, mesh.shape["space"], mesh.shape["tm"]),
        mesh=mesh,
        in_specs=(P("tm", None, "space"), P("tm", "space"), P("tm", "space")),
        out_specs=P("tm", None, "space"),
        check_vma=False,
    )
```

time: 210 us -> 44.9 us (0.21)
  other arithmetic: 88.7 us -> 0 us
  waiting for transfers between devices: 57.6 us -> 0 us
  Pallas kernels: 0 us -> 40.9 us
  matrix products: 40.1 us -> 0 us
  between operations: 13.5 us -> 0.03 us
  blocking collectives: 9.3 us -> 0 us
  local copies, waits for them, and re-layouts: 0.35 us -> 3.62 us
    another operation x6 -> x0, other arithmetic: 86.7 us -> none  [the longest x3 47.1 us: transform(): factor = jnp.linalg.cholesky(spread_dof * identity + gram_total)]
    psum x1 -> x0, waiting for transfers between devices: 57.6 us -> none  [per_device(): summed = lax.psum(gram_part, 'space')]
    pallas_call x0 -> x3, Pallas kernels: none -> 40.9 us  [the longest x1 28.9 us: per_device(): pl.pallas_call(functools.partial(chain_kernel, space, tm, times, steps),...]
    dot_general x14 -> x0, matrix products: 39.5 us -> none  [the longest x1 31.2 us: per_device(): jnp.einsum('tmo,tno->tmn', scaled, scaled, preferred_element_type=jnp.flo...]
    all_gather x1 -> x0, blocking collectives: 9.3 us -> none  [carried_in(): gathered = lax.all_gather(part, axis)]
    unnamed x0 -> x8, local copies, waits for them, and re-layouts: none -> 3.62 us
  transfers between devices with their start and end apart: 1 -> 0, of which waited for: 1 -> 0; matrix products, arithmetic and copies ran while one was open for 0% -> 0% of each run, Pallas kernels for 0% -> 0%
where the time goes in v1:
time: 44.9 us; the launch traced here: 44.5 us
  Pallas kernels  40.9 us (91%)
  local copies, waits for them, and re-layouts  3.62 us (8%)
    pallas_call x1, Pallas kernels, per_device(): pl.pallas_call(functools.partial(chain_kernel, space, tm, times, steps),...  28.9 us
    pallas_call x1, Pallas kernels, per_device(): pl.pallas_call(gram_kernel, grid=(times,), in_specs=[one_time, whole_vmem...  8.73 us
    unnamed x8, local copies, waits for them, and re-layouts  3.62 us
    pallas_call x1, Pallas kernels, per_device(): pl.pallas_call(smooth_kernel, grid=(times,), in_specs=[square, one_time],...  3.25 us

profile of v1, /device:TPU:0, one launch (start us, length us, event | category | flops | bytes accessed | tf_op | source)
XLA Modules:
  0.0 44.5 jit_solution(14123730350996276993)
XLA Ops:
  0.0 0.0 copy-start
  0.0 2.2 %copy-done = bf16[4,128,4096]{2,1,0:T(8,128)(2,1)S(1)} copy-done((bf16[4,128,4096]{2,1,0:T(8,128)(2,1)S(1)}, bf16[4,128,4096]{2,1,0:T(8,128)(2,1)}, u32[]{:S(2)}) %copy-start) | copy-done | bytes 4194328
  2.2 0.0 copy-start.2
  2.2 0.7 %copy-done.2 = s32[4,1024]{1,0:T(4,128)S(1)} copy-done((s32[4,1024]{1,0:T(4,128)S(1)}, s32[4,1024]{1,0:T(4,128)}, u32[]{:S(2)}) %copy-start.2) | copy-done | bytes 16408
  2.9 0.0 copy-start.3
  2.9 0.7 %copy-done.3 = f32[4,1024]{1,0:T(4,128)S(1)} copy-done((f32[4,1024]{1,0:T(4,128)S(1)}, f32[4,1024]{1,0:T(4,128)}, u32[]{:S(2)}) %copy-start.3) | copy-done | bytes 16408
  3.6 0.0 copy-start.1
  3.6 8.7 %shard_map.37 = f32[4,128,128]{2,1,0:T(8,128)S(1)} custom-call(bf16[4,128,4096]{2,1,0:T(8,128)(2,1)S(1)} %copy-done, s32[4,1024]{1,0:T(4,128)S(1)} %copy-done.2, f32[4,1024]{1,0:T(4,128)S(1)} %copy-done.3), custom_call_target="tpu_custom_call" | custom-call | tf_op jit(solution)/shard_map/pallas_call | solution.py:229
  12.4 28.9 %shard_map.38.chain_ref = bf16[4,128,128]{2,1,0:T(8,128)(2,1)S(1)} custom-call(f32[512,128]{1,0:T(8,128)S(1)} %bitcast.1), custom_call_target="tpu_custom_call" | custom-call | tf_op jit(solution)/shard_map/pallas_call | solution.py:243
  41.3 0.0 copy-done.1
  41.3 3.2 %shard_map.39 = bf16[4,128,4096]{2,1,0:T(8,128)(2,1)} custom-call(bf16[4,128,128]{2,1,0:T(8,128)(2,1)S(1)} %shard_map.38.chain_ref, bf16[4,128,4096]{2,1,0:T(8,128)(2,1)S(1)} %copy-done.1), custom_call_target="tpu_custom_call" | custom-call | tf_op jit(solution)/shard_map/pallas_call | solution.py:263
Async XLA Ops:
  0.0 2.2 %copy-start = (bf16[4,128,4096]{2,1,0:T(8,128)(2,1)S(1)}, bf16[4,128,4096]{2,1,0:T(8,128)(2,1)}, u32[]{:S(2)}) copy-start(bf16[4,128,4096]{2,1,0:T(8,128)(2,1)} %anomalies_ref.3) | copy-start | bytes 12582916
  2.2 0.7 %copy-start.2 = (s32[4,1024]{1,0:T(4,128)S(1)}, s32[4,1024]{1,0:T(4,128)}, u32[]{:S(2)}) copy-start(s32[4,1024]{1,0:T(4,128)} %index_ref.1) | copy-start | bytes 49156
  2.9 0.7 %copy-start.3 = (f32[4,1024]{1,0:T(4,128)S(1)}, f32[4,1024]{1,0:T(4,128)}, u32[]{:S(2)}) copy-start(f32[4,1024]{1,0:T(4,128)} %weight_ref.1) | copy-start | bytes 49156
  3.6 37.7 %copy-start.1 = (bf16[4,128,4096]{2,1,0:T(8,128)(2,1)S(1)}, bf16[4,128,4096]{2,1,0:T(8,128)(2,1)}, u32[]{:S(2)}) copy-start(bf16[4,128,4096]{2,1,0:T(8,128)(2,1)} %anomalies_ref.3) | copy-start | bytes 12582916

commit v2 on v1

--- a/solution.py
+++ b/solution.py
@@ -9,13 +9,30 @@
 from jax.sharding import PartitionSpec as P
 
 MESH = pl.DeviceIdType.MESH
-HIGHEST = lax.Precision.HIGHEST
 GROUPS = 4
 LARGEST_SCALED = 51.0 * 0.12
 
 
+def split(value):
+    high = value.astype(jnp.bfloat16)
+    rest = value - high.astype(jnp.float32)
+    middle = rest.astype(jnp.bfloat16)
+    low = (rest - middle.astype(jnp.float32)).astype(jnp.bfloat16)
+    return high, middle, low
+
+
 def exact_dot(left, right):
-    return jnp.dot(left, right, precision=HIGHEST, preferred_element_type=jnp.float32)
+    width = right.shape[1]
+    left_high, left_middle, left_low = split(left)
+    right_high, right_middle, right_low = split(right)
+    main_left = jnp.concatenate([left_high, left_middle], axis=1)
+    main_row = jnp.concatenate([right_high, right_middle], axis=1)
+    main_right = jnp.concatenate([main_row, main_row], axis=0)
+    rest_left = jnp.concatenate([left_high, left_low], axis=1)
+    rest_right = jnp.concatenate([right_low, right_high], axis=0)
+    main = jnp.dot(main_left, main_right, preferred_element_type=jnp.float32)
+    rest = jnp.dot(rest_left, rest_right, preferred_element_type=jnp.float32)
+    return main[:, :width] + (main[:, width:] + rest)
 
 
 def gram_kernel(anomalies_ref, index_ref, weight_ref, gram_ref):
@@ -236,7 +253,7 @@
     )(anomalies, obs_index, obs_weight)
 
     bound = 1.0 + members * obs * space * LARGEST_SCALED**2 / (members - 1)
-    steps = math.ceil(math.log(bound / 4.0, 4)) + 4
+    steps = math.ceil(math.log(bound / 4.0, 4)) + 3
     rows = times * members // space
     team = space // times
     dma = pltpu.SemaphoreType.DMA

time: 44.9 us -> 44.1 us (0.982)
  Pallas kernels: 40.9 us -> 40.2 us
    pallas_call x1, Pallas kernels: 28.9 us -> 28.2 us  [per_device(): pl.pallas_call(functools.partial(chain_kernel, space, tm, times, steps),...]
where the time goes in v2:
time: 44.1 us; the launch traced here: 43.8 us
  Pallas kernels  40.2 us (91%)
  local copies, waits for them, and re-layouts  3.62 us (8%)
    pallas_call x1, Pallas kernels, per_device(): pl.pallas_call(functools.partial(chain_kernel, space, tm, times, steps),...  28.2 us
    pallas_call x1, Pallas kernels, per_device(): pl.pallas_call(gram_kernel, grid=(times,), in_specs=[one_time, whole_vmem...  8.73 us
    unnamed x8, local copies, waits for them, and re-layouts  3.62 us
    pallas_call x1, Pallas kernels, per_device(): pl.pallas_call(smooth_kernel, grid=(times,), in_specs=[square, one_time],...  3.25 us

profile of v2, /device:TPU:0, one launch (start us, length us, event | category | flops | bytes accessed | tf_op | source)
XLA Modules:
  0.0 43.8 jit_solution(6202209695110689526)
XLA Ops:
  0.0 0.0 copy-start
  0.0 2.2 %copy-done = bf16[4,128,4096]{2,1,0:T(8,128)(2,1)S(1)} copy-done((bf16[4,128,4096]{2,1,0:T(8,128)(2,1)S(1)}, bf16[4,128,4096]{2,1,0:T(8,128)(2,1)}, u32[]{:S(2)}) %copy-start) | copy-done | bytes 4194328
  2.2 0.0 copy-start.2
  2.2 0.7 %copy-done.2 = s32[4,1024]{1,0:T(4,128)S(1)} copy-done((s32[4,1024]{1,0:T(4,128)S(1)}, s32[4,1024]{1,0:T(4,128)}, u32[]{:S(2)}) %copy-start.2) | copy-done | bytes 16408
  2.9 0.0 copy-start.3
  2.9 0.7 %copy-done.3 = f32[4,1024]{1,0:T(4,128)S(1)} copy-done((f32[4,1024]{1,0:T(4,128)S(1)}, f32[4,1024]{1,0:T(4,128)}, u32[]{:S(2)}) %copy-start.3) | copy-done | bytes 16408
  3.6 0.0 copy-start.1
  3.6 8.7 %shard_map.37 = f32[4,128,128]{2,1,0:T(8,128)S(1)} custom-call(bf16[4,128,4096]{2,1,0:T(8,128)(2,1)S(1)} %copy-done, s32[4,1024]{1,0:T(4,128)S(1)} %copy-done.2, f32[4,1024]{1,0:T(4,128)S(1)} %copy-done.3), custom_call_target="tpu_custom_call" | custom-call | tf_op jit(solution)/shard_map/pallas_call | solution.py:246
  12.4 28.2 %shard_map.38.chain_ref = bf16[4,128,128]{2,1,0:T(8,128)(2,1)S(1)} custom-call(f32[512,128]{1,0:T(8,128)S(1)} %bitcast.1), custom_call_target="tpu_custom_call" | custom-call | tf_op jit(solution)/shard_map/pallas_call | solution.py:260
  40.5 0.0 copy-done.1
  40.6 3.2 %shard_map.39 = bf16[4,128,4096]{2,1,0:T(8,128)(2,1)} custom-call(bf16[4,128,128]{2,1,0:T(8,128)(2,1)S(1)} %shard_map.38.chain_ref, bf16[4,128,4096]{2,1,0:T(8,128)(2,1)S(1)} %copy-done.1), custom_call_target="tpu_custom_call" | custom-call | tf_op jit(solution)/shard_map/pallas_call | solution.py:280
Async XLA Ops:
  0.0 2.2 %copy-start = (bf16[4,128,4096]{2,1,0:T(8,128)(2,1)S(1)}, bf16[4,128,4096]{2,1,0:T(8,128)(2,1)}, u32[]{:S(2)}) copy-start(bf16[4,128,4096]{2,1,0:T(8,128)(2,1)} %anomalies_ref.3) | copy-start | bytes 12582916
  2.2 0.7 %copy-start.2 = (s32[4,1024]{1,0:T(4,128)S(1)}, s32[4,1024]{1,0:T(4,128)}, u32[]{:S(2)}) copy-start(s32[4,1024]{1,0:T(4,128)} %index_ref.1) | copy-start | bytes 49156
  2.9 0.7 %copy-start.3 = (f32[4,1024]{1,0:T(4,128)S(1)}, f32[4,1024]{1,0:T(4,128)}, u32[]{:S(2)}) copy-start(f32[4,1024]{1,0:T(4,128)} %weight_ref.1) | copy-start | bytes 49156
  3.6 36.9 %copy-start.1 = (bf16[4,128,4096]{2,1,0:T(8,128)(2,1)S(1)}, bf16[4,128,4096]{2,1,0:T(8,128)(2,1)}, u32[]{:S(2)}) copy-start(bf16[4,128,4096]{2,1,0:T(8,128)(2,1)} %anomalies_ref.3) | copy-start | bytes 12582916

commit v3 on v2

--- a/solution.py
+++ b/solution.py
@@ -35,19 +35,16 @@
     return main[:, :width] + (main[:, width:] + rest)
 
 
-def gram_kernel(anomalies_ref, index_ref, weight_ref, gram_ref):
-    time = pl.program_id(0)
-    members, cells = anomalies_ref.shape[1:]
-    obs = index_ref.shape[1]
+def gram_of(cells_at, index, weight):
+    members, cells = cells_at.shape
+    obs = index.shape[1]
     span = cells // GROUPS
     shift = span.bit_length() - 1
     chunk = 256 if obs % 256 == 0 else obs
-    index = index_ref[pl.ds(time, 1), :]
-    weight = weight_ref[pl.ds(time, 1), :]
     low = jnp.bitwise_and(index, span - 1)
     high = lax.shift_right_logical(index, shift)
     stacked = jnp.concatenate(
-        [anomalies_ref[0, :, g * span:(g + 1) * span] for g in range(GROUPS)], axis=0
+        [cells_at[:, g * span:(g + 1) * span] for g in range(GROUPS)], axis=0
     )
     cell_ids = lax.broadcasted_iota(jnp.int32, (span, chunk), 0)
     total = jnp.zeros((members, members), jnp.float32)
@@ -63,7 +60,7 @@
         total = total + lax.dot_general(
             scaled, scaled, (((1,), (1,)), ((), ())), preferred_element_type=jnp.float32
         )
-    gram_ref[0] = total
+    return total
 
 
 def inverse_of(matrix, identity, steps, both_ref):
@@ -90,9 +87,12 @@
     return items[0]
 
 
-def chain_kernel(space, tm, times, steps, gram_ref, out_ref, landed, matrix, weights, products, both_ref,
-                 scatter_send, scatter_recv, share_send, share_recv, spread_send, spread_recv,
-                 pass_send, pass_recv, time_send, time_recv, relay_send, relay_recv):
+def chain_kernel(space, tm, times, steps, anomalies_ref, index_ref, weight_ref, out_ref,
+                 cells, index, weight, gram, landed, partner, matrix, weights, products, both_ref,
+                 load_sem, index_sem, weight_sem,
+                 scatter_send, scatter_recv, partner_send, partner_recv, share_send, share_recv,
+                 spread_send, spread_recv, pass_send, pass_recv, time_send, time_recv,
+                 relay_send, relay_recv):
     members = matrix.shape[0]
     me = lax.axis_index("space")
     mine = lax.axis_index("tm")
@@ -111,44 +111,74 @@
             device_id=device, device_id_type=MESH,
         )
 
+    order = [(owned + 1 + i) % times for i in range(times)]
+    index_load = pltpu.make_async_copy(index_ref, index, index_sem)
+    weight_load = pltpu.make_async_copy(weight_ref, weight, weight_sem)
+    loads = [
+        pltpu.make_async_copy(anomalies_ref.at[slot], cells.at[i], load_sem.at[i])
+        for i, slot in enumerate(order)
+    ]
+    index_load.start()
+    loads[0].start()
+    weight_load.start()
+    for load in loads[1:]:
+        load.start()
+
     barrier = pltpu.get_barrier_semaphore()
     for d in range(1, space):
         pl.semaphore_signal(barrier, inc=1, device_id={"space": (me + d) % space}, device_id_type=MESH)
     for d in range(1, tm):
         pl.semaphore_signal(barrier, inc=1, device_id={"tm": (mine + d) % tm}, device_id_type=MESH)
-    pl.semaphore_wait(barrier, space + tm - 2)
+    index_load.wait()
+    weight_load.wait()
 
     sends = []
-    for d in range(1, space):
-        peer = (me + d) % space
-        copy = to(gram_ref.at[row_slice(peer)], landed.at[d], scatter_send.at[d],
-                  scatter_recv.at[d], space=peer)
+    for i, slot in enumerate(order):
+        loads[i].wait()
+        gram[slot] = gram_of(cells.at[i], index[pl.ds(slot, 1), :], weight[pl.ds(slot, 1), :])
+        if i == 0:
+            pl.semaphore_wait(barrier, space + tm - 2)
+        if i < times - 1:
+            for e in range(team):
+                peer = (place + e) % team
+                copy = to(gram.at[slot, row_slice(peer)], landed.at[i, e], scatter_send.at[i, e],
+                          scatter_recv.at[i, e], space=slot * team + peer)
+                copy.start()
+                sends.append(copy)
+    partners = []
+    for e in range(1, team):
+        copy = to(gram.at[owned], partner.at[e], partner_send.at[e], partner_recv.at[e],
+                  space=base + (place + e) % team)
         copy.start()
-        sends.append(copy)
+        partners.append(copy)
     for copy in sends:
         copy.wait_recv()
-    total = gram_ref[row_slice(me), :]
-    for d in range(1, space):
-        total = total + landed[d]
-    matrix[row_slice(place), :] = total
+    matrix[row_slice(place), :] = jnp.sum(
+        landed[...].reshape((times - 1) * team, rows, members), axis=0
+    )
     shares = []
-    for d in range(1, team):
-        peer = (place + d) % team
-        copy = to(matrix.at[row_slice(place)], matrix.at[row_slice(place)], share_send.at[d],
-                  share_recv.at[d], space=base + peer)
+    for e in range(1, team):
+        copy = to(matrix.at[row_slice(place)], matrix.at[row_slice(place)], share_send.at[e],
+                  share_recv.at[e], space=base + (place + e) % team)
         copy.start()
         shares.append(copy)
-    for d in range(1, team):
-        origin = (place + team - d) % team
-        to(matrix.at[row_slice(origin)], matrix.at[row_slice(origin)], share_send.at[d],
-           share_recv.at[d], space=base + origin).wait_recv()
+    total = gram[owned]
+    for copy in partners:
+        copy.wait_recv()
+    for e in range(1, team):
+        total = total + partner[e]
+    for e in range(1, team):
+        origin = (place + team - e) % team
+        to(matrix.at[row_slice(origin)], matrix.at[row_slice(origin)], share_send.at[e],
+           share_recv.at[e], space=base + origin).wait_recv()
+    total = total + matrix[...]
 
     identity = (
         lax.broadcasted_iota(jnp.int32, (members, members), 0)
         == lax.broadcasted_iota(jnp.int32, (members, members), 1)
     ).astype(jnp.float32)
     spread = float(members - 1)
-    weights[owned] = inverse_of(identity + matrix[...] / spread, identity, steps, both_ref)
+    weights[owned] = inverse_of(identity + total / spread, identity, steps, both_ref)
 
     def own_rows(slot):
         return weights.at[slot, row_slice(place)]
@@ -215,7 +245,7 @@
     for t in range(times):
         out_ref[t] = chains[t * members:(t + 1) * members].T.astype(out_ref.dtype)
 
-    for copy in sends + shares:
+    for copy in sends + shares + partners:
         copy.wait_send()
     for d in range(1, tm):
         @pl.when(mine >= d)
@@ -243,39 +273,40 @@
     whole_vmem = pl.BlockSpec(memory_space=pltpu.VMEM)
     one_time = pl.BlockSpec((1, members, cells), lambda t: (t, 0, 0))
     square = pl.BlockSpec((1, members, members), lambda t: (t, 0, 0))
-    gram = pl.pallas_call(
-        gram_kernel,
-        grid=(times,),
-        in_specs=[one_time, whole_vmem, whole_vmem],
-        out_specs=square,
-        out_shape=jax.ShapeDtypeStruct((times, members, members), jnp.float32),
-        compiler_params=pltpu.CompilerParams(vmem_limit_bytes=40 * 2**20),
-    )(anomalies, obs_index, obs_weight)
-
     bound = 1.0 + members * obs * space * LARGEST_SCALED**2 / (members - 1)
     steps = math.ceil(math.log(bound / 4.0, 4)) + 3
     rows = times * members // space
     team = space // times
     dma = pltpu.SemaphoreType.DMA
+    in_hbm = pl.BlockSpec(memory_space=pltpu.HBM)
+    wide = jnp.float32
+    square_wide = (members, members)
     chains = pl.pallas_call(
         functools.partial(chain_kernel, space, tm, times, steps),
-        in_specs=[whole_vmem],
+        in_specs=[in_hbm] * 3,
         out_specs=whole_vmem,
         out_shape=jax.ShapeDtypeStruct((times, members, members), jnp.bfloat16),
         scratch_shapes=[
-            pltpu.VMEM((space, rows, members), jnp.float32),
-            pltpu.VMEM((members, members), jnp.float32),
-            pltpu.VMEM((times, members, members), jnp.float32),
-            pltpu.VMEM((tm, members, members), jnp.float32),
-            pltpu.VMEM((2 * members, members), jnp.float32),
-            dma((space,)), dma((space,)), dma((team,)), dma((team,)), dma((times,)), dma((times,)),
+            pltpu.VMEM(anomalies.shape, anomalies.dtype),
+            pltpu.VMEM(obs_index.shape, obs_index.dtype),
+            pltpu.VMEM(obs_weight.shape, obs_weight.dtype),
+            pltpu.VMEM((times, *square_wide), wide),
+            pltpu.VMEM((times - 1, team, rows, members), wide),
+            pltpu.VMEM((team, *square_wide), wide),
+            pltpu.VMEM(square_wide, wide),
+            pltpu.VMEM((times, *square_wide), wide),
+            pltpu.VMEM((tm, *square_wide), wide),
+            pltpu.VMEM((2 * members, members), wide),
+            dma((times,)), dma, dma,
+            dma((times, team)), dma((times, team)), dma((team,)), dma((team,)),
+            dma((team,)), dma((team,)), dma((times,)), dma((times,)),
             dma((times, team)), dma((times, team)), dma((tm,)), dma((tm,)),
             dma((tm, team)), dma((tm, team)),
         ],
         compiler_params=pltpu.CompilerParams(
-            collective_id=0, has_side_effects=True, vmem_limit_bytes=40 * 2**20
+            collective_id=0, has_side_effects=True, vmem_limit_bytes=63 * 2**20
         ),
-    )(gram.reshape(times * members, members))
+    )(anomalies, obs_index, obs_weight)
 
     return pl.pallas_call(
         smooth_kernel,

time: 44.1 us -> 38 us (0.86)
  Pallas kernels: 40.2 us -> 34.6 us
  local copies, waits for them, and re-layouts: 3.62 us -> 3.09 us
    pallas_call x1 -> x0, Pallas kernels: 8.73 us -> none  [per_device(): pl.pallas_call(gram_kernel, grid=(times,), in_specs=[one_time, whole_vmem...]
    pallas_call x1, Pallas kernels: 28.2 us -> 31.4 us  [per_device(): pl.pallas_call(functools.partial(chain_kernel, space, tm, times, steps),...]
    unnamed x8 -> x4, local copies, waits for them, and re-layouts: 3.62 us -> 3.09 us
where the time goes in v3:
time: 38 us; the launch traced here: 37.7 us
  Pallas kernels  34.6 us (91%)
  local copies, waits for them, and re-layouts  3.09 us (8%)
    pallas_call x1, Pallas kernels, per_device(): pl.pallas_call(functools.partial(chain_kernel, space, tm, times, steps),...  31.4 us
    pallas_call x1, Pallas kernels, per_device(): pl.pallas_call(smooth_kernel, grid=(times,), in_specs=[square, one_time],...  3.22 us
    unnamed x4, local copies, waits for them, and re-layouts  3.09 us

profile of v3, /device:TPU:0, one launch (start us, length us, event | category | flops | bytes accessed | tf_op | source)
XLA Modules:
  0.0 37.7 jit_solution(3783968916962996891)
XLA Ops:
  0.0 31.4 %shard_map.37.chain_ref = bf16[4,128,128]{2,1,0:T(8,128)(2,1)} custom-call(bf16[4,128,4096]{2,1,0:T(8,128)(2,1)} %anomalies_ref.3, s32[4,1024]{1,0:T(4,128)} %index_ref.1, f32[4,1024]{1,0:T(4,128)} %weight_ref.1), custom_call_target="tpu_custom_call" | custom-call | tf_op jit(solution)/shard_map/pallas_call | solution.py:284
  31.4 0.0 copy-start
  31.4 2.2 %copy-done = bf16[4,128,4096]{2,1,0:T(8,128)(2,1)S(1)} copy-done((bf16[4,128,4096]{2,1,0:T(8,128)(2,1)S(1)}, bf16[4,128,4096]{2,1,0:T(8,128)(2,1)}, u32[]{:S(2)}) %copy-start) | copy-done | bytes 4194328
  33.6 0.0 copy-start.1
  33.6 0.9 %copy-done.1 = bf16[4,128,128]{2,1,0:T(8,128)(2,1)S(1)} copy-done((bf16[4,128,128]{2,1,0:T(8,128)(2,1)S(1)}, bf16[4,128,128]{2,1,0:T(8,128)(2,1)}, u32[]{:S(2)}) %copy-start.1) | copy-done | bytes 131096
  34.5 3.2 %shard_map.38 = bf16[4,128,4096]{2,1,0:T(8,128)(2,1)} custom-call(bf16[4,128,128]{2,1,0:T(8,128)(2,1)S(1)} %copy-done.1, bf16[4,128,4096]{2,1,0:T(8,128)(2,1)S(1)} %copy-done), custom_call_target="tpu_custom_call" | custom-call | tf_op jit(solution)/shard_map/pallas_call | solution.py:311
Async XLA Ops:
  31.4 2.2 %copy-start = (bf16[4,128,4096]{2,1,0:T(8,128)(2,1)S(1)}, bf16[4,128,4096]{2,1,0:T(8,128)(2,1)}, u32[]{:S(2)}) copy-start(bf16[4,128,4096]{2,1,0:T(8,128)(2,1)} %anomalies_ref.3) | copy-start | bytes 12582916
  33.6 0.9 %copy-start.1 = (bf16[4,128,128]{2,1,0:T(8,128)(2,1)S(1)}, bf16[4,128,128]{2,1,0:T(8,128)(2,1)}, u32[]{:S(2)}) copy-start(bf16[4,128,128]{2,1,0:T(8,128)(2,1)} %shard_map.37.chain_ref) | copy-start | bytes 393220

commit v4 on v3

--- a/solution.py
+++ b/solution.py
@@ -88,7 +88,7 @@
 
 
 def chain_kernel(space, tm, times, steps, anomalies_ref, index_ref, weight_ref, out_ref,
-                 cells, index, weight, gram, landed, partner, matrix, weights, products, both_ref,
+                 cells, index, weight, gram, landed, partner, matrix, weights, products, both_ref, chains_ref,
                  load_sem, index_sem, weight_sem,
                  scatter_send, scatter_recv, partner_send, partner_recv, share_send, share_recv,
                  spread_send, spread_recv, pass_send, pass_recv, time_send, time_recv,
@@ -230,6 +230,7 @@
             for e in range(1, team):
                 to(product_rows(slot, place), product_rows(slot, place), relay_send.at[d, e],
                    relay_recv.at[d, e], space=base + (place + e) % team).start()
+    chains_ref[...] = jnp.concatenate(tails, axis=0)
     for d in range(1, tm):
         @pl.when(mine + d < tm)
         def _(d=d):
@@ -238,12 +239,10 @@
                 origin = (place + team - e) % team
                 to(product_rows(slot, origin), product_rows(slot, origin), relay_send.at[d, e],
                    relay_recv.at[d, e], space=base + origin).wait_recv()
-
-    later = [jnp.where(slot > mine, products[slot], identity) for slot in range(1, tm)]
-    suffix = tree(later) if later else identity
-    chains = exact_dot(jnp.concatenate(tails, axis=0), suffix)
+            chains_ref[...] = exact_dot(chains_ref[...], products[slot])
+
     for t in range(times):
-        out_ref[t] = chains[t * members:(t + 1) * members].T.astype(out_ref.dtype)
+        out_ref[t] = chains_ref[t * members:(t + 1) * members].T.astype(out_ref.dtype)
 
     for copy in sends + shares + partners:
         copy.wait_send()
@@ -271,8 +270,7 @@
     times, members, cells = anomalies.shape
     obs = obs_index.shape[1]
     whole_vmem = pl.BlockSpec(memory_space=pltpu.VMEM)
-    one_time = pl.BlockSpec((1, members, cells), lambda t: (t, 0, 0))
-    square = pl.BlockSpec((1, members, members), lambda t: (t, 0, 0))
+
     bound = 1.0 + members * obs * space * LARGEST_SCALED**2 / (members - 1)
     steps = math.ceil(math.log(bound / 4.0, 4)) + 3
     rows = times * members // space
@@ -297,6 +295,7 @@
             pltpu.VMEM((times, *square_wide), wide),
             pltpu.VMEM((tm, *square_wide), wide),
             pltpu.VMEM((2 * members, members), wide),
+            pltpu.VMEM((times * members, members), wide),
             dma((times,)), dma, dma,
             dma((times, team)), dma((times, team)), dma((team,)), dma((team,)),
             dma((team,)), dma((team,)), dma((times,)), dma((times,)),
@@ -308,13 +307,15 @@
         ),
     )(anomalies, obs_index, obs_weight)
 
+    tiles = 2
+    tile = pl.BlockSpec((1, members, cells // tiles), lambda t, c: (t, 0, c))
     return pl.pallas_call(
         smooth_kernel,
-        grid=(times,),
-        in_specs=[square, one_time],
-        out_specs=one_time,
+        grid=(times, tiles),
+        in_specs=[pl.BlockSpec((1, members, members), lambda t, c: (t, 0, 0)), tile],
+        out_specs=tile,
         out_shape=jax.ShapeDtypeStruct(anomalies.shape, anomalies.dtype),
-        compiler_params=pltpu.CompilerParams(vmem_limit_bytes=40 * 2**20),
+        compiler_params=pltpu.CompilerParams(vmem_limit_bytes=63 * 2**20),
     )(chains, anomalies)
 
 

time: 38 us -> 39 us (1.026)
  Pallas kernels: 34.6 us -> 38.7 us
  local copies, waits for them, and re-layouts: 3.09 us -> 0 us
    pallas_call x1, Pallas kernels: 3.22 us -> 7.55 us  [per_device(): pl.pallas_call(smooth_kernel, grid=(times, tiles), in_specs=[pl.BlockSpec...]
    unnamed x4 -> x0, local copies, waits for them, and re-layouts: 3.09 us -> none
where the time goes in v4:
time: 39 us; the launch traced here: 38.7 us
  Pallas kernels  38.7 us (99%)
    pallas_call x1, Pallas kernels, per_device(): pl.pallas_call(functools.partial(chain_kernel, space, tm, times, steps),...  31.1 us
    pallas_call x1, Pallas kernels, per_device(): pl.pallas_call(smooth_kernel, grid=(times, tiles), in_specs=[pl.BlockSpec...  7.55 us

profile of v4, /device:TPU:0, one launch (start us, length us, event | category | flops | bytes accessed | tf_op | source)
XLA Modules:
  0.0 38.7 jit_solution(11449128535747754006)
XLA Ops:
  0.0 31.1 %shard_map.37.chain_ref = bf16[4,128,128]{2,1,0:T(8,128)(2,1)} custom-call(bf16[4,128,4096]{2,1,0:T(8,128)(2,1)} %anomalies_ref.3, s32[4,1024]{1,0:T(4,128)} %index_ref.1, f32[4,1024]{1,0:T(4,128)} %weight_ref.1), custom_call_target="tpu_custom_call" | custom-call | tf_op jit(solution)/shard_map/pallas_call | solution.py:282
  31.1 7.5 %shard_map.38 = bf16[4,128,4096]{2,1,0:T(8,128)(2,1)} custom-call(bf16[4,128,128]{2,1,0:T(8,128)(2,1)} %shard_map.37.chain_ref, bf16[4,128,4096]{2,1,0:T(8,128)(2,1)} %anomalies_ref.3), custom_call_target="tpu_custom_call" | custom-call | tf_op jit(solution)/shard_map/pallas_call | solution.py:312

commit v5 on v4

--- a/solution.py
+++ b/solution.py
@@ -260,10 +260,24 @@
                    relay_recv.at[d, e], space=base + (place + e) % team).wait_send()
 
 
-def smooth_kernel(chain_ref, anomalies_ref, out_ref):
-    out_ref[0] = jnp.dot(
-        chain_ref[0], anomalies_ref[0], preferred_element_type=jnp.float32
-    ).astype(out_ref.dtype)
+def smooth_kernel(chain_ref, anomalies_ref, out_ref, done, done_sem):
+    times, members, cells = anomalies_ref.shape
+    parts = done_sem.shape[1]
+    width = cells // parts
+    copies = []
+    for t in range(times):
+        for c in range(parts):
+            part = slice(c * width, (c + 1) * width)
+            done[t, :, part] = jnp.dot(
+                chain_ref[t], anomalies_ref[t, :, part], preferred_element_type=jnp.float32
+            ).astype(done.dtype)
+            copy = pltpu.make_async_copy(
+                done.at[t, :, part], out_ref.at[t, :, part], done_sem.at[t, c]
+            )
+            copy.start()
+            copies.append(copy)
+    for copy in copies:
+        copy.wait()
 
 
 def per_device(space, tm, anomalies, obs_index, obs_weight):
@@ -303,19 +317,17 @@
             dma((tm, team)), dma((tm, team)),
         ],
         compiler_params=pltpu.CompilerParams(
-            collective_id=0, has_side_effects=True, vmem_limit_bytes=63 * 2**20
+            collective_id=0, has_side_effects=True, vmem_limit_bytes=40 * 2**20
         ),
-    )(anomalies, obs_index, obs_weight)
-
-    tiles = 2
-    tile = pl.BlockSpec((1, members, cells // tiles), lambda t, c: (t, 0, c))
+    )(*(pltpu.with_memory_space_constraint(x, pltpu.HBM) for x in (anomalies, obs_index, obs_weight)))
+
     return pl.pallas_call(
         smooth_kernel,
-        grid=(times, tiles),
-        in_specs=[pl.BlockSpec((1, members, members), lambda t, c: (t, 0, 0)), tile],
-        out_specs=tile,
+        in_specs=[whole_vmem, whole_vmem],
+        out_specs=in_hbm,
         out_shape=jax.ShapeDtypeStruct(anomalies.shape, anomalies.dtype),
-        compiler_params=pltpu.CompilerParams(vmem_limit_bytes=63 * 2**20),
+        scratch_shapes=[pltpu.VMEM(anomalies.shape, anomalies.dtype), dma((times, 2))],
+        compiler_params=pltpu.CompilerParams(vmem_limit_bytes=40 * 2**20),
     )(chains, anomalies)
 
 

time: 39 us -> 32.8 us (0.84)
  Pallas kernels: 38.7 us -> 32.6 us
    pallas_call x1, Pallas kernels: 7.55 us -> 2.36 us  [per_device(): pl.pallas_call(smooth_kernel, in_specs=[whole_vmem, whole_vmem], out_spec...]
    pallas_call x1, Pallas kernels: 31.1 us -> 30.3 us  [per_device(): pl.pallas_call(functools.partial(chain_kernel, space, tm, times, steps),...]
where the time goes in v5:
time: 32.8 us; the launch traced here: 32.7 us
  Pallas kernels  32.6 us (99%)
    pallas_call x1, Pallas kernels, per_device(): pl.pallas_call(functools.partial(chain_kernel, space, tm, times, steps),...  30.3 us
    pallas_call x1, Pallas kernels, per_device(): pl.pallas_call(smooth_kernel, in_specs=[whole_vmem, whole_vmem], out_spec...  2.36 us

profile of v5, /device:TPU:0, one launch (start us, length us, event | category | flops | bytes accessed | tf_op | source)
XLA Modules:
  0.0 32.7 jit_solution(1968658098228638325)
XLA Ops:
  0.0 0.0 copy-start
  0.0 30.3 %shard_map.37.chain_ref = bf16[4,128,128]{2,1,0:T(8,128)(2,1)S(1)} custom-call(bf16[4,128,4096]{2,1,0:T(8,128)(2,1)} %anomalies_ref.3, s32[4,1024]{1,0:T(4,128)} %index_ref.1, f32[4,1024]{1,0:T(4,128)} %weight_ref.1), custom_call_target="tpu_custom_call" | custom-call | tf_op jit(solution)/shard_map/pallas_call | solution.py:296
  30.3 0.0 copy-done
  30.3 2.4 %shard_map.38 = bf16[4,128,4096]{2,1,0:T(8,128)(2,1)} custom-call(bf16[4,128,128]{2,1,0:T(8,128)(2,1)S(1)} %shard_map.37.chain_ref, bf16[4,128,4096]{2,1,0:T(8,128)(2,1)S(1)} %copy-done), custom_call_target="tpu_custom_call" | custom-call | tf_op jit(solution)/shard_map/pallas_call | solution.py:324
Async XLA Ops:
  0.0 30.3 %copy-start = (bf16[4,128,4096]{2,1,0:T(8,128)(2,1)S(1)}, bf16[4,128,4096]{2,1,0:T(8,128)(2,1)}, u32[]{:S(2)}) copy-start(bf16[4,128,4096]{2,1,0:T(8,128)(2,1)} %anomalies_ref.3) | copy-start | bytes 12582916

commit v6 on v5

--- a/solution.py
+++ b/solution.py
@@ -9,7 +9,7 @@
 from jax.sharding import PartitionSpec as P
 
 MESH = pl.DeviceIdType.MESH
-GROUPS = 4
+LANES = 128
 LARGEST_SCALED = 51.0 * 0.12
 
 
@@ -35,32 +35,38 @@
     return main[:, :width] + (main[:, width:] + rest)
 
 
-def gram_of(cells_at, index, weight):
-    members, cells = cells_at.shape
+def cell_roots(index, weight, cells):
+    low = jnp.bitwise_and(index, LANES - 1)
+    high = lax.shift_right_logical(index, LANES.bit_length() - 1)
+    groups = cells // LANES
     obs = index.shape[1]
-    span = cells // GROUPS
-    shift = span.bit_length() - 1
-    chunk = 256 if obs % 256 == 0 else obs
-    low = jnp.bitwise_and(index, span - 1)
-    high = lax.shift_right_logical(index, shift)
-    stacked = jnp.concatenate(
-        [cells_at[:, g * span:(g + 1) * span] for g in range(GROUPS)], axis=0
-    )
-    cell_ids = lax.broadcasted_iota(jnp.int32, (span, chunk), 0)
-    total = jnp.zeros((members, members), jnp.float32)
-    for start in range(0, obs, chunk):
-        part = slice(start, start + chunk)
-        selector = (cell_ids == low[:, part]).astype(jnp.float32).astype(jnp.bfloat16)
-        picked = jnp.dot(stacked, selector, preferred_element_type=jnp.float32)
-        scaled = jnp.zeros((members, chunk), jnp.float32)
-        for g in range(GROUPS):
-            group_weight = jnp.where(high[:, part] == g, weight[:, part], 0.0)
-            scaled = scaled + picked[g * members:(g + 1) * members] * group_weight
-        scaled = scaled.astype(jnp.bfloat16)
-        total = total + lax.dot_general(
-            scaled, scaled, (((1,), (1,)), ((), ())), preferred_element_type=jnp.float32
-        )
-    return total
+    square = weight * weight
+    coarse = square.astype(jnp.bfloat16).astype(jnp.float32)
+    in_group = lax.broadcasted_iota(jnp.int32, (groups, obs), 0) == high
+    left = jnp.concatenate(
+        [jnp.where(in_group, coarse, 0.0), jnp.where(in_group, square - coarse, 0.0)], axis=0
+    ).astype(jnp.bfloat16)
+    right = (lax.broadcasted_iota(jnp.int32, (LANES, obs), 0) == low)
+    right = right.astype(jnp.float32).astype(jnp.bfloat16)
+    both = lax.dot_general(
+        left, right, (((1,), (1,)), ((), ())), preferred_element_type=jnp.float32
+    )
+    return jnp.sqrt(both[:groups] + both[groups:])
+
+
+def gram_of(cells_at, roots):
+    groups = roots.shape[0]
+    scaled = jnp.concatenate(
+        [
+            (cells_at[:, g * LANES:(g + 1) * LANES].astype(jnp.float32) * roots[g:g + 1])
+            .astype(jnp.bfloat16)
+            for g in range(groups)
+        ],
+        axis=1,
+    )
+    return lax.dot_general(
+        scaled, scaled, (((1,), (1,)), ((), ())), preferred_element_type=jnp.float32
+    )
 
 
 def inverse_of(matrix, identity, steps, both_ref):
@@ -133,9 +139,13 @@
     weight_load.wait()
 
     sends = []
+    roots = [
+        cell_roots(index[pl.ds(slot, 1), :], weight[pl.ds(slot, 1), :], cells.shape[2])
+        for slot in order
+    ]
     for i, slot in enumerate(order):
         loads[i].wait()
-        gram[slot] = gram_of(cells.at[i], index[pl.ds(slot, 1), :], weight[pl.ds(slot, 1), :])
+        gram[slot] = gram_of(cells.at[i], roots[i])
         if i == 0:
             pl.semaphore_wait(barrier, space + tm - 2)
         if i < times - 1:

time: 32.8 us -> 30.8 us (0.939)
  Pallas kernels: 32.6 us -> 30.6 us
    pallas_call x1, Pallas kernels: 30.3 us -> 28.2 us  [per_device(): pl.pallas_call(functools.partial(chain_kernel, space, tm, times, steps),...]
where the time goes in v6:
time: 30.8 us; the launch traced here: 30.6 us
  Pallas kernels  30.6 us (99%)
    pallas_call x1, Pallas kernels, per_device(): pl.pallas_call(functools.partial(chain_kernel, space, tm, times, steps),...  28.2 us
    pallas_call x1, Pallas kernels, per_device(): pl.pallas_call(smooth_kernel, in_specs=[whole_vmem, whole_vmem], out_spec...  2.36 us

profile of v6, /device:TPU:0, one launch (start us, length us, event | category | flops | bytes accessed | tf_op | source)
XLA Modules:
  0.0 30.6 jit_solution(13472867763453640488)
XLA Ops:
  0.0 0.0 copy-start
  0.0 28.2 %shard_map.37.chain_ref = bf16[4,128,128]{2,1,0:T(8,128)(2,1)S(1)} custom-call(bf16[4,128,4096]{2,1,0:T(8,128)(2,1)} %anomalies_ref.3, s32[4,1024]{1,0:T(4,128)} %index_ref.1, f32[4,1024]{1,0:T(4,128)} %weight_ref.1), custom_call_target="tpu_custom_call" | custom-call | tf_op jit(solution)/shard_map/pallas_call | solution.py:306
  28.3 0.0 copy-done
  28.3 2.4 %shard_map.38 = bf16[4,128,4096]{2,1,0:T(8,128)(2,1)} custom-call(bf16[4,128,128]{2,1,0:T(8,128)(2,1)S(1)} %shard_map.37.chain_ref, bf16[4,128,4096]{2,1,0:T(8,128)(2,1)S(1)} %copy-done), custom_call_target="tpu_custom_call" | custom-call | tf_op jit(solution)/shard_map/pallas_call | solution.py:334
Async XLA Ops:
  0.0 28.3 %copy-start = (bf16[4,128,4096]{2,1,0:T(8,128)(2,1)S(1)}, bf16[4,128,4096]{2,1,0:T(8,128)(2,1)}, u32[]{:S(2)}) copy-start(bf16[4,128,4096]{2,1,0:T(8,128)(2,1)} %anomalies_ref.3) | copy-start | bytes 12582916

commit v7 on v6

--- a/solution.py
+++ b/solution.py
@@ -94,9 +94,9 @@
 
 
 def chain_kernel(space, tm, times, steps, anomalies_ref, index_ref, weight_ref, out_ref,
-                 cells, index, weight, gram, landed, partner, matrix, weights, products, both_ref, chains_ref,
+                 cells, index, weight, gram, near, joint, far, partner, matrix, weights, products, both_ref, chains_ref,
                  load_sem, index_sem, weight_sem,
-                 scatter_send, scatter_recv, partner_send, partner_recv, share_send, share_recv,
+                 near_send, near_recv, far_send, far_recv, partner_send, partner_recv, share_send, share_recv,
                  spread_send, spread_recv, pass_send, pass_recv, time_send, time_recv,
                  relay_send, relay_recv):
     members = matrix.shape[0]
@@ -139,6 +139,21 @@
     weight_load.wait()
 
     sends = []
+    near_copies = []
+    far_copies = []
+
+    def pass_on(i):
+        piece = gram[order[i], row_slice(place), :]
+        for copy in near_copies[i]:
+            copy.wait_recv()
+        for e in range(1, team):
+            piece = piece + near[i, e]
+        joint[i] = piece
+        copy = to(joint.at[i], far.at[i], far_send.at[i], far_recv.at[i],
+                  space=order[i] * team + place)
+        copy.start()
+        far_copies.append(copy)
+
     roots = [
         cell_roots(index[pl.ds(slot, 1), :], weight[pl.ds(slot, 1), :], cells.shape[2])
         for slot in order
@@ -149,23 +164,26 @@
         if i == 0:
             pl.semaphore_wait(barrier, space + tm - 2)
         if i < times - 1:
-            for e in range(team):
+            near_copies.append([])
+            for e in range(1, team):
                 peer = (place + e) % team
-                copy = to(gram.at[slot, row_slice(peer)], landed.at[i, e], scatter_send.at[i, e],
-                          scatter_recv.at[i, e], space=slot * team + peer)
+                copy = to(gram.at[slot, row_slice(peer)], near.at[i, e], near_send.at[i, e],
+                          near_recv.at[i, e], space=base + peer)
                 copy.start()
-                sends.append(copy)
+                near_copies[i].append(copy)
+        if 2 <= i < times - 1:
+            pass_on(i - 2)
     partners = []
     for e in range(1, team):
         copy = to(gram.at[owned], partner.at[e], partner_send.at[e], partner_recv.at[e],
                   space=base + (place + e) % team)
         copy.start()
         partners.append(copy)
-    for copy in sends:
+    for i in range(max(times - 3, 0), times - 1):
+        pass_on(i)
+    for copy in far_copies:
         copy.wait_recv()
-    matrix[row_slice(place), :] = jnp.sum(
-        landed[...].reshape((times - 1) * team, rows, members), axis=0
-    )
+    matrix[row_slice(place), :] = jnp.sum(far[...], axis=0)
     shares = []
     for e in range(1, team):
         copy = to(matrix.at[row_slice(place)], matrix.at[row_slice(place)], share_send.at[e],
@@ -254,7 +272,7 @@
     for t in range(times):
         out_ref[t] = chains_ref[t * members:(t + 1) * members].T.astype(out_ref.dtype)
 
-    for copy in sends + shares + partners:
+    for copy in sum(near_copies, sends + shares + partners + far_copies):
         copy.wait_send()
     for d in range(1, tm):
         @pl.when(mine >= d)
@@ -314,6 +332,8 @@
             pltpu.VMEM(obs_weight.shape, obs_weight.dtype),
             pltpu.VMEM((times, *square_wide), wide),
             pltpu.VMEM((times - 1, team, rows, members), wide),
+            pltpu.VMEM((times - 1, rows, members), wide),
+            pltpu.VMEM((times - 1, rows, members), wide),
             pltpu.VMEM((team, *square_wide), wide),
             pltpu.VMEM(square_wide, wide),
             pltpu.VMEM((times, *square_wide), wide),
@@ -321,7 +341,7 @@
             pltpu.VMEM((2 * members, members), wide),
             pltpu.VMEM((times * members, members), wide),
             dma((times,)), dma, dma,
-            dma((times, team)), dma((times, team)), dma((team,)), dma((team,)),
+            dma((times, team)), dma((times, team)), dma((times,)), dma((times,)), dma((team,)), dma((team,)),
             dma((team,)), dma((team,)), dma((times,)), dma((times,)),
             dma((times, team)), dma((times, team)), dma((tm,)), dma((tm,)),
             dma((tm, team)), dma((tm, team)),

time: 30.8 us -> 30.5 us (level)
  no operation moved by 1% of the time
where the time goes in v7:
time: 30.5 us; the launch traced here: 30.3 us
  Pallas kernels  30.3 us (99%)
    pallas_call x1, Pallas kernels, per_device(): pl.pallas_call(functools.partial(chain_kernel, space, tm, times, steps),...  28 us
    pallas_call x1, Pallas kernels, per_device(): pl.pallas_call(smooth_kernel, in_specs=[whole_vmem, whole_vmem], out_spec...  2.36 us

profile of v7, /device:TPU:0, one launch (start us, length us, event | category | flops | bytes accessed | tf_op | source)
XLA Modules:
  0.0 30.3 jit_solution(15814336821841946385)
XLA Ops:
  0.0 0.0 copy-start
  0.0 28.0 %shard_map.37.chain_ref = bf16[4,128,128]{2,1,0:T(8,128)(2,1)S(1)} custom-call(bf16[4,128,4096]{2,1,0:T(8,128)(2,1)} %anomalies_ref.3, s32[4,1024]{1,0:T(4,128)} %index_ref.1, f32[4,1024]{1,0:T(4,128)} %weight_ref.1), custom_call_target="tpu_custom_call" | custom-call | tf_op jit(solution)/shard_map/pallas_call | solution.py:324
  28.0 0.0 copy-done
  28.0 2.4 %shard_map.38 = bf16[4,128,4096]{2,1,0:T(8,128)(2,1)} custom-call(bf16[4,128,128]{2,1,0:T(8,128)(2,1)S(1)} %shard_map.37.chain_ref, bf16[4,128,4096]{2,1,0:T(8,128)(2,1)S(1)} %copy-done), custom_call_target="tpu_custom_call" | custom-call | tf_op jit(solution)/shard_map/pallas_call | solution.py:354
Async XLA Ops:
  0.0 28.0 %copy-start = (bf16[4,128,4096]{2,1,0:T(8,128)(2,1)S(1)}, bf16[4,128,4096]{2,1,0:T(8,128)(2,1)}, u32[]{:S(2)}) copy-start(bf16[4,128,4096]{2,1,0:T(8,128)(2,1)} %anomalies_ref.3) | copy-start | bytes 12582916

commit v8 on v7

--- a/solution.py
+++ b/solution.py
@@ -16,15 +16,26 @@
 def split(value):
     high = value.astype(jnp.bfloat16)
     rest = value - high.astype(jnp.float32)
-    middle = rest.astype(jnp.bfloat16)
-    low = (rest - middle.astype(jnp.float32)).astype(jnp.bfloat16)
-    return high, middle, low
+    return high, rest.astype(jnp.bfloat16), rest
+
+
+def near_dot(left, right):
+    width = right.shape[1]
+    left_high, left_middle, _ = split(left)
+    right_high, right_middle, _ = split(right)
+    main_left = jnp.concatenate([left_high, left_middle], axis=1)
+    main_row = jnp.concatenate([right_high, right_middle], axis=1)
+    main_right = jnp.concatenate([main_row, main_row], axis=0)
+    main = jnp.dot(main_left, main_right, preferred_element_type=jnp.float32)
+    return main[:, :width] + main[:, width:]
 
 
 def exact_dot(left, right):
     width = right.shape[1]
-    left_high, left_middle, left_low = split(left)
-    right_high, right_middle, right_low = split(right)
+    left_high, left_middle, left_rest = split(left)
+    right_high, right_middle, right_rest = split(right)
+    left_low = (left_rest - left_middle.astype(jnp.float32)).astype(jnp.bfloat16)
+    right_low = (right_rest - right_middle.astype(jnp.float32)).astype(jnp.bfloat16)
     main_left = jnp.concatenate([left_high, left_middle], axis=1)
     main_row = jnp.concatenate([right_high, right_middle], axis=1)
     main_right = jnp.concatenate([main_row, main_row], axis=0)
@@ -69,32 +80,37 @@
     )
 
 
-def inverse_of(matrix, identity, steps, both_ref):
-    norm = jnp.max(jnp.sum(jnp.abs(matrix), axis=1, keepdims=True), axis=0, keepdims=True)
-    least = 1.0 / norm
+def inverse_of(matrix, identity, steps):
     size = matrix.shape[0]
-    both_ref[:size] = matrix * least
-    both_ref[size:] = identity * least
-
-    def step(_, least):
+    norm = jnp.max(jnp.sum(jnp.abs(matrix), axis=0, keepdims=True), axis=1, keepdims=True)
+    least = jnp.broadcast_to(1.0 / norm, (1, size))
+    own = matrix * least
+    result = identity * least
+    for step in range(steps):
         alpha = 2.0 / (1.0 + least)
-        factor = (2.0 * alpha) * identity - (alpha * alpha) * both_ref[:size]
-        both_ref[...] = exact_dot(both_ref[...], factor)
-        return 4.0 * least / ((1.0 + least) * (1.0 + least))
-
-    lax.fori_loop(0, steps, step, least)
-    return both_ref[size:]
+        factor = (2.0 * alpha) * identity - (alpha * alpha) * own
+        dot = exact_dot if step < steps - 5 else near_dot
+        if step == 0:
+            result = factor * least
+            own = dot(own, factor)
+        elif step == steps - 1:
+            result = dot(result, factor)
+        else:
+            both = dot(jnp.concatenate([own, result], axis=0), factor)
+            own, result = both[:size], both[size:]
+        least = (alpha * alpha) * least
+    return result
 
 
 def tree(items):
     while len(items) > 1:
-        paired = [exact_dot(a, b) for a, b in zip(items[::2], items[1::2])]
+        paired = [near_dot(a, b) for a, b in zip(items[::2], items[1::2])]
         items = paired + items[len(items) - len(items) % 2:]
     return items[0]
 
 
 def chain_kernel(space, tm, times, steps, anomalies_ref, index_ref, weight_ref, out_ref,
-                 cells, index, weight, gram, near, joint, far, partner, matrix, weights, products, both_ref, chains_ref,
+                 cells, index, weight, gram, near, joint, far, partner, matrix, weights, products, chains_ref,
                  load_sem, index_sem, weight_sem,
                  near_send, near_recv, far_send, far_recv, partner_send, partner_recv, share_send, share_recv,
                  spread_send, spread_recv, pass_send, pass_recv, time_send, time_recv,
@@ -206,7 +222,7 @@
         == lax.broadcasted_iota(jnp.int32, (members, members), 1)
     ).astype(jnp.float32)
     spread = float(members - 1)
-    weights[owned] = inverse_of(identity + total / spread, identity, steps, both_ref)
+    weights[owned] = inverse_of(identity + total / spread, identity, steps)
 
     def own_rows(slot):
         return weights.at[slot, row_slice(place)]
@@ -246,7 +262,7 @@
 
     tails = [identity]
     for t in range(times - 1, 0, -1):
-        tails.append(exact_dot(each[t], tails[-1]) if t < times - 1 else each[t])
+        tails.append(near_dot(each[t], tails[-1]) if t < times - 1 else each[t])
     tails = tails[::-1]
 
     for d in range(1, tm):
@@ -267,7 +283,7 @@
                 origin = (place + team - e) % team
                 to(product_rows(slot, origin), product_rows(slot, origin), relay_send.at[d, e],
                    relay_recv.at[d, e], space=base + origin).wait_recv()
-            chains_ref[...] = exact_dot(chains_ref[...], products[slot])
+            chains_ref[...] = near_dot(chains_ref[...], products[slot])
 
     for t in range(times):
         out_ref[t] = chains_ref[t * members:(t + 1) * members].T.astype(out_ref.dtype)
@@ -338,7 +354,6 @@
             pltpu.VMEM(square_wide, wide),
             pltpu.VMEM((times, *square_wide), wide),
             pltpu.VMEM((tm, *square_wide), wide),
-            pltpu.VMEM((2 * members, members), wide),
             pltpu.VMEM((times * members, members), wide),
             dma((times,)), dma, dma,
             dma((times, team)), dma((times, team)), dma((times,)), dma((times,)), dma((team,)), dma((team,)),

time: 30.5 us -> 29.6 us (0.970)
  Pallas kernels: 30.3 us -> 29.4 us
    pallas_call x1, Pallas kernels: 28 us -> 27 us  [per_device(): pl.pallas_call(functools.partial(chain_kernel, space, tm, times, steps),...]
where the time goes in v8:
time: 29.6 us; the launch traced here: 29.4 us
  Pallas kernels  29.4 us (99%)
    pallas_call x1, Pallas kernels, per_device(): pl.pallas_call(functools.partial(chain_kernel, space, tm, times, steps),...  27 us
    pallas_call x1, Pallas kernels, per_device(): pl.pallas_call(smooth_kernel, in_specs=[whole_vmem, whole_vmem], out_spec...  2.36 us

profile of v8, /device:TPU:0, one launch (start us, length us, event | category | flops | bytes accessed | tf_op | source)
XLA Modules:
  0.0 29.4 jit_solution(6451217497386261466)
XLA Ops:
  0.0 0.0 copy-start
  0.0 27.0 %shard_map.37.chain_ref = bf16[4,128,128]{2,1,0:T(8,128)(2,1)S(1)} custom-call(bf16[4,128,4096]{2,1,0:T(8,128)(2,1)} %anomalies_ref.3, s32[4,1024]{1,0:T(4,128)} %index_ref.1, f32[4,1024]{1,0:T(4,128)} %weight_ref.1), custom_call_target="tpu_custom_call" | custom-call | tf_op jit(solution)/shard_map/pallas_call | solution.py:340
  27.0 0.0 copy-done
  27.0 2.4 %shard_map.38 = bf16[4,128,4096]{2,1,0:T(8,128)(2,1)} custom-call(bf16[4,128,128]{2,1,0:T(8,128)(2,1)S(1)} %shard_map.37.chain_ref, bf16[4,128,4096]{2,1,0:T(8,128)(2,1)S(1)} %copy-done), custom_call_target="tpu_custom_call" | custom-call | tf_op jit(solution)/shard_map/pallas_call | solution.py:369
Async XLA Ops:
  0.0 27.0 %copy-start = (bf16[4,128,4096]{2,1,0:T(8,128)(2,1)S(1)}, bf16[4,128,4096]{2,1,0:T(8,128)(2,1)}, u32[]{:S(2)}) copy-start(bf16[4,128,4096]{2,1,0:T(8,128)(2,1)} %anomalies_ref.3) | copy-start | bytes 12582916

commit v9 on v8

--- a/solution.py
+++ b/solution.py
@@ -113,8 +113,7 @@
                  cells, index, weight, gram, near, joint, far, partner, matrix, weights, products, chains_ref,
                  load_sem, index_sem, weight_sem,
                  near_send, near_recv, far_send, far_recv, partner_send, partner_recv, share_send, share_recv,
-                 spread_send, spread_recv, pass_send, pass_recv, time_send, time_recv,
-                 relay_send, relay_recv):
+                 spread_send, spread_recv, pass_send, pass_recv, time_send, time_recv):
     members = matrix.shape[0]
     me = lax.axis_index("space")
     mine = lax.axis_index("tm")
@@ -251,38 +250,24 @@
     each = [weights[t] for t in range(times)]
     products[mine] = tree(each)
 
-    def product_rows(slot, number):
-        return products.at[slot, row_slice(number)]
-
     for d in range(1, tm):
         @pl.when(mine >= d)
         def _(d=d):
-            to(product_rows(mine, place), product_rows(mine, place), time_send.at[d],
-               time_recv.at[d], tm=jnp.maximum(mine - d, 0)).start()
+            to(products.at[mine], products.at[mine], time_send.at[d], time_recv.at[d],
+               tm=jnp.maximum(mine - d, 0)).start()
 
     tails = [identity]
     for t in range(times - 1, 0, -1):
         tails.append(near_dot(each[t], tails[-1]) if t < times - 1 else each[t])
     tails = tails[::-1]
 
-    for d in range(1, tm):
-        @pl.when(mine + d < tm)
-        def _(d=d):
-            slot = jnp.minimum(mine + d, tm - 1)
-            to(product_rows(slot, place), product_rows(slot, place), time_send.at[d],
-               time_recv.at[d], tm=slot).wait_recv()
-            for e in range(1, team):
-                to(product_rows(slot, place), product_rows(slot, place), relay_send.at[d, e],
-                   relay_recv.at[d, e], space=base + (place + e) % team).start()
     chains_ref[...] = jnp.concatenate(tails, axis=0)
     for d in range(1, tm):
         @pl.when(mine + d < tm)
         def _(d=d):
             slot = jnp.minimum(mine + d, tm - 1)
-            for e in range(1, team):
-                origin = (place + team - e) % team
-                to(product_rows(slot, origin), product_rows(slot, origin), relay_send.at[d, e],
-                   relay_recv.at[d, e], space=base + origin).wait_recv()
+            to(products.at[slot], products.at[slot], time_send.at[d], time_recv.at[d],
+               tm=slot).wait_recv()
             chains_ref[...] = near_dot(chains_ref[...], products[slot])
 
     for t in range(times):
@@ -293,15 +278,8 @@
     for d in range(1, tm):
         @pl.when(mine >= d)
         def _(d=d):
-            to(product_rows(mine, place), product_rows(mine, place), time_send.at[d],
-               time_recv.at[d], tm=jnp.maximum(mine - d, 0)).wait_send()
-
-        @pl.when(mine + d < tm)
-        def _(d=d):
-            slot = jnp.minimum(mine + d, tm - 1)
-            for e in range(1, team):
-                to(product_rows(slot, place), product_rows(slot, place), relay_send.at[d, e],
-                   relay_recv.at[d, e], space=base + (place + e) % team).wait_send()
+            to(products.at[mine], products.at[mine], time_send.at[d], time_recv.at[d],
+               tm=jnp.maximum(mine - d, 0)).wait_send()
 
 
 def smooth_kernel(chain_ref, anomalies_ref, out_ref, done, done_sem):
@@ -359,7 +337,6 @@
             dma((times, team)), dma((times, team)), dma((times,)), dma((times,)), dma((team,)), dma((team,)),
             dma((team,)), dma((team,)), dma((times,)), dma((times,)),
             dma((times, team)), dma((times, team)), dma((tm,)), dma((tm,)),
-            dma((tm, team)), dma((tm, team)),
         ],
         compiler_params=pltpu.CompilerParams(
             collective_id=0, has_side_effects=True, vmem_limit_bytes=40 * 2**20

time: 29.6 us -> 30.1 us (1.017)
  Pallas kernels: 29.4 us -> 29.9 us
    pallas_call x1, Pallas kernels: 27 us -> 27.6 us  [per_device(): pl.pallas_call(functools.partial(chain_kernel, space, tm, times, steps),...]
where the time goes in v9:
time: 30.1 us; the launch traced here: 29.9 us
  Pallas kernels  29.9 us (99%)
    pallas_call x1, Pallas kernels, per_device(): pl.pallas_call(functools.partial(chain_kernel, space, tm, times, steps),...  27.6 us
    pallas_call x1, Pallas kernels, per_device(): pl.pallas_call(smooth_kernel, in_specs=[whole_vmem, whole_vmem], out_spec...  2.36 us

profile of v9, /device:TPU:0, one launch (start us, length us, event | category | flops | bytes accessed | tf_op | source)
XLA Modules:
  0.0 29.9 jit_solution(7611487989617985042)
XLA Ops:
  0.0 0.0 copy-start
  0.0 27.6 %shard_map.37.chain_ref = bf16[4,128,128]{2,1,0:T(8,128)(2,1)S(1)} custom-call(bf16[4,128,4096]{2,1,0:T(8,128)(2,1)} %anomalies_ref.3, s32[4,1024]{1,0:T(4,128)} %index_ref.1, f32[4,1024]{1,0:T(4,128)} %weight_ref.1), custom_call_target="tpu_custom_call" | custom-call | tf_op jit(solution)/shard_map/pallas_call | solution.py:318
  27.6 0.0 copy-done
  27.6 2.4 %shard_map.38 = bf16[4,128,4096]{2,1,0:T(8,128)(2,1)} custom-call(bf16[4,128,128]{2,1,0:T(8,128)(2,1)S(1)} %shard_map.37.chain_ref, bf16[4,128,4096]{2,1,0:T(8,128)(2,1)S(1)} %copy-done), custom_call_target="tpu_custom_call" | custom-call | tf_op jit(solution)/shard_map/pallas_call | solution.py:346
Async XLA Ops:
  0.0 27.6 %copy-start = (bf16[4,128,4096]{2,1,0:T(8,128)(2,1)S(1)}, bf16[4,128,4096]{2,1,0:T(8,128)(2,1)}, u32[]{:S(2)}) copy-start(bf16[4,128,4096]{2,1,0:T(8,128)(2,1)} %anomalies_ref.3) | copy-start | bytes 12582916

commit v10 on v8

--- a/solution.py
+++ b/solution.py
@@ -89,7 +89,7 @@
     for step in range(steps):
         alpha = 2.0 / (1.0 + least)
         factor = (2.0 * alpha) * identity - (alpha * alpha) * own
-        dot = exact_dot if step < steps - 5 else near_dot
+        dot = exact_dot if step < steps - 7 else near_dot
         if step == 0:
             result = factor * least
             own = dot(own, factor)
@@ -254,7 +254,7 @@
     def product_rows(slot, number):
         return products.at[slot, row_slice(number)]
 
-    for d in range(1, tm):
+    for d in range(tm - 1, 0, -1):
         @pl.when(mine >= d)
         def _(d=d):
             to(product_rows(mine, place), product_rows(mine, place), time_send.at[d],

time: 29.6 us -> 29 us (0.980)
  Pallas kernels: 29.4 us -> 28.6 us
    pallas_call x1, Pallas kernels: 27 us -> 26.3 us  [per_device(): pl.pallas_call(functools.partial(chain_kernel, space, tm, times, steps),...]
where the time goes in v10:
time: 29 us; the launch traced here: 28.6 us
  Pallas kernels  28.6 us (99%)
    pallas_call x1, Pallas kernels, per_device(): pl.pallas_call(functools.partial(chain_kernel, space, tm, times, steps),...  26.3 us
    pallas_call x1, Pallas kernels, per_device(): pl.pallas_call(smooth_kernel, in_specs=[whole_vmem, whole_vmem], out_spec...  2.35 us

profile of v10, /device:TPU:0, one launch (start us, length us, event | category | flops | bytes accessed | tf_op | source)
XLA Modules:
  0.0 28.6 jit_solution(2619725688008660656)
XLA Ops:
  0.0 0.0 copy-start
  0.0 26.3 %shard_map.37.chain_ref = bf16[4,128,128]{2,1,0:T(8,128)(2,1)S(1)} custom-call(bf16[4,128,4096]{2,1,0:T(8,128)(2,1)} %anomalies_ref.3, s32[4,1024]{1,0:T(4,128)} %index_ref.1, f32[4,1024]{1,0:T(4,128)} %weight_ref.1), custom_call_target="tpu_custom_call" | custom-call | tf_op jit(solution)/shard_map/pallas_call | solution.py:340
  26.3 0.0 copy-done
  26.3 2.4 %shard_map.38 = bf16[4,128,4096]{2,1,0:T(8,128)(2,1)} custom-call(bf16[4,128,128]{2,1,0:T(8,128)(2,1)S(1)} %shard_map.37.chain_ref, bf16[4,128,4096]{2,1,0:T(8,128)(2,1)S(1)} %copy-done), custom_call_target="tpu_custom_call" | custom-call | tf_op jit(solution)/shard_map/pallas_call | solution.py:369
Async XLA Ops:
  0.0 26.3 %copy-start = (bf16[4,128,4096]{2,1,0:T(8,128)(2,1)S(1)}, bf16[4,128,4096]{2,1,0:T(8,128)(2,1)}, u32[]{:S(2)}) copy-start(bf16[4,128,4096]{2,1,0:T(8,128)(2,1)} %anomalies_ref.3) | copy-start | bytes 12582916

commit v11 on v10

--- a/solution.py
+++ b/solution.py
@@ -227,7 +227,7 @@
     def own_rows(slot):
         return weights.at[slot, row_slice(place)]
 
-    for d in range(1, times):
+    for d in sorted(range(1, times), key=lambda d: abs(2 * d - times)):
         copy = to(own_rows(owned), own_rows(owned), spread_send.at[d], spread_recv.at[d],
                   space=((owned + d) % times) * team + place)
         copy.start()
@@ -249,7 +249,10 @@
             to(there, there, pass_send.at[d, e], pass_recv.at[d, e], space=base + origin).wait_recv()
 
     each = [weights[t] for t in range(times)]
-    products[mine] = tree(each)
+
+    @pl.when(mine > 0)
+    def _():
+        products[mine] = tree(each)
 
     def product_rows(slot, number):
         return products.at[slot, row_slice(number)]

time: 29 us -> 29.9 us (1.031)
  Pallas kernels: 28.6 us -> 29.5 us
    pallas_call x1, Pallas kernels: 26.3 us -> 27.1 us  [per_device(): pl.pallas_call(functools.partial(chain_kernel, space, tm, times, steps),...]
where the time goes in v11:
time: 29.9 us; the launch traced here: 29.5 us
  Pallas kernels  29.5 us (99%)
    pallas_call x1, Pallas kernels, per_device(): pl.pallas_call(functools.partial(chain_kernel, space, tm, times, steps),...  27.1 us
    pallas_call x1, Pallas kernels, per_device(): pl.pallas_call(smooth_kernel, in_specs=[whole_vmem, whole_vmem], out_spec...  2.36 us

profile of v11, /device:TPU:0, one launch (start us, length us, event | category | flops | bytes accessed | tf_op | source)
XLA Modules:
  0.0 29.5 jit_solution(16608945044209576413)
XLA Ops:
  0.0 0.0 copy-start
  0.0 27.1 %shard_map.37.chain_ref = bf16[4,128,128]{2,1,0:T(8,128)(2,1)S(1)} custom-call(bf16[4,128,4096]{2,1,0:T(8,128)(2,1)} %anomalies_ref.3, s32[4,1024]{1,0:T(4,128)} %index_ref.1, f32[4,1024]{1,0:T(4,128)} %weight_ref.1), custom_call_target="tpu_custom_call" | custom-call | tf_op jit(solution)/shard_map/pallas_call | solution.py:343
  27.1 0.0 copy-done
  27.1 2.4 %shard_map.38 = bf16[4,128,4096]{2,1,0:T(8,128)(2,1)} custom-call(bf16[4,128,128]{2,1,0:T(8,128)(2,1)S(1)} %shard_map.37.chain_ref, bf16[4,128,4096]{2,1,0:T(8,128)(2,1)S(1)} %copy-done), custom_call_target="tpu_custom_call" | custom-call | tf_op jit(solution)/shard_map/pallas_call | solution.py:372
Async XLA Ops:
  0.0 27.1 %copy-start = (bf16[4,128,4096]{2,1,0:T(8,128)(2,1)S(1)}, bf16[4,128,4096]{2,1,0:T(8,128)(2,1)}, u32[]{:S(2)}) copy-start(bf16[4,128,4096]{2,1,0:T(8,128)(2,1)} %anomalies_ref.3) | copy-start | bytes 12582916
